TPU v7x, 128 devices: a whole 4x4x4 slice. The times are simulated.
128 devices in a mesh: image: 4 (over x), context: 16 (over y, z_lo, core), dp: 2 (over z_hi).
Axes of the slice: x: 4, y: 4, z: 4 (z_hi: 2, z_lo: 2; z = z_hi * 2 + z_lo), core: 2. Of those that a mesh axis runs over, the one named last changes fastest.
Arguments:
- text: bfloat16 [8192, 8192], P(('context', 'dp'), 'image'), may hold values from -6 to 6
- patches: bfloat16 [8, 1024, 8192], P('image', ('context', 'dp')), may hold values from -6 to 6
- in_gain: float32 [8192], replicated, may hold values from 0.25 to 1.75
- q_weight: bfloat16 [8192, 4096], P('dp', 'image'), may hold values from -0.0625 to 0.0625
- k_weight: bfloat16 [8192, 512], P('dp', 'image'), may hold values from -0.0625 to 0.0625
- v_weight: bfloat16 [8192, 512], P('dp', 'image'), may hold values from -0.0625 to 0.0625
- o_weight: bfloat16 [4096, 8192], P('image', 'dp'), may hold values from -0.09375 to 0.09375
- q_gain: float32 [128], replicated, may hold values from 1 to 32
- k_gain: float32 [128], replicated, may hold values from 1 to 32
- gate: float32 [1], replicated, may hold values from 0.4 to 1.5
- block_mask: int32 [64, 8], P(('context', 'dp')), may hold values from 0 to 1, as said below
- owner_ids: int32 [8], replicated, may hold values from 0 to 7, each once
Outputs:
- mixed: bfloat16 [8192, 8192], P(('context', 'dp'), 'image')
Inputs may be any that keep to these rules, and one draw needn't show every extreme that they name: `block_mask`: every text block reads at least one image. `owner_ids`: a permutation of the image numbers.
All inputs are finite; a program needn't handle non-finite values.
Results may differ from a plain program's by a relative error of at most 0.017.
The roundings to bfloat16 on the way count: a program that leaves them out, or rounds other values in their place, can miss the bound.
Values may be sent and summed in bfloat16 or wider, within the bound.
A program may use at most 192 MiB of HBM per device.

v0:
```python
import jax
import jax.numpy as jnp
from jax import lax
from jax.sharding import PartitionSpec as P

D = 8192
HD = 128
BLOCK = 128


def rms_scale(values, gain):
    mean_square = jnp.mean(values * values, axis=-1, keepdims=True)
    return values * lax.rsqrt(mean_square + 1e-05) * gain


def local(
    text,
    patches,
    in_gain,
    q_weight,
    k_weight,
    v_weight,
    o_weight,
    q_gain,
    k_gain,
    gate,
    block_mask,
    owner_ids,
):
    tok_count = text.shape[0]
    whole = lax.all_gather(text, "image", axis=1, tiled=True)
    normed = rms_scale(whole.astype(jnp.float32), in_gain).astype(jnp.bfloat16)
    query_cols = q_weight.shape[1]
    columns = normed
    queries = jnp.dot(
        columns,
        lax.all_gather(q_weight, "dp", axis=0, tiled=True),
        preferred_element_type=jnp.float32,
    )
    heads_local = query_cols // HD
    queries = rms_scale(queries.reshape(tok_count, heads_local, HD), q_gain).astype(jnp.bfloat16)
    all_patches = lax.all_gather(patches, "image", axis=0, tiled=True)
    image_count = all_patches.shape[0]
    patch_count = all_patches.shape[1]
    flat_rows = all_patches.reshape(image_count * patch_count, D)
    kv_cols = k_weight.shape[1]
    kv_local = kv_cols // HD
    pieces = (
        lax.all_gather(k_weight, "dp", axis=0, tiled=True),
        lax.all_gather(v_weight, "dp", axis=0, tiled=True),
    )
    columns = flat_rows
    key_sum = jnp.dot(columns, pieces[0], preferred_element_type=jnp.float32)
    value_sum = jnp.dot(columns, pieces[1], preferred_element_type=jnp.float32)
    keys = rms_scale(key_sum.reshape(image_count, patch_count, kv_local, HD), k_gain).astype(
        jnp.bfloat16
    )
    keys = keys.reshape(image_count, patch_count, kv_cols)
    values = value_sum.astype(jnp.bfloat16).reshape(image_count, patch_count, kv_cols)
    onehot = (owner_ids[:, None] == jnp.arange(image_count, dtype=jnp.int32)[None, :]).astype(
        jnp.int32
    )
    readable = jnp.sum(block_mask[:, None, :] * onehot[None, :, :], axis=2) > 0
    row_read = jnp.repeat(readable, BLOCK, axis=0)
    group = heads_local // kv_local
    by_group = jnp.transpose(queries.reshape(tok_count, kv_local, group, HD), (2, 0, 1, 3))
    scale = 1.0 / HD**0.5
    row_mask = row_read[None, :, :, None]
    start_state = (
        jnp.full((group, kv_local, tok_count), -1e30, jnp.float32),
        jnp.zeros((group, kv_local, tok_count), jnp.float32),
        jnp.zeros((group, kv_local, tok_count, HD), jnp.float32),
    )
    pieces = (
        lax.all_gather(keys, ("context", "dp"), axis=1, tiled=True),
        lax.all_gather(values, ("context", "dp"), axis=1, tiled=True),
    )
    piece_rows = pieces[0].shape[1]
    key_piece = pieces[0].reshape(image_count, piece_rows, kv_local, HD)
    value_piece = pieces[1].reshape(image_count, piece_rows, kv_local, HD)

    def one_group(inputs):
        group_queries, running_max, running_total, running_sum = inputs
        scores = (
            jnp.einsum(
                "tjd,irjd->jtir", group_queries, key_piece, preferred_element_type=jnp.float32
            )
            * scale
        )
        scores = jnp.where(row_mask, scores, -1e30)
        new_max = jnp.maximum(running_max, jnp.max(scores, axis=(2, 3)))
        weights = jnp.where(row_mask, jnp.exp(scores - new_max[:, :, None, None]), 0.0)
        factor = jnp.exp(running_max - new_max)
        new_total = running_total * factor + jnp.sum(weights, axis=(2, 3))
        rounded = weights.astype(jnp.bfloat16)
        added = jnp.einsum(
            "jtir,irjd->jtd", rounded, value_piece, preferred_element_type=jnp.float32
        )
        new_sum = running_sum * factor[:, :, None] + added
        return (new_max, new_total, new_sum)

    final_state = lax.map(one_group, (by_group, start_state[0], start_state[1], start_state[2]))
    attended = final_state[2] / final_state[1][:, :, :, None]
    attended = (
        jnp.transpose(attended, (2, 1, 0, 3))
        .reshape(tok_count, heads_local * HD)
        .astype(jnp.bfloat16)
    )
    projected = jnp.dot(
        attended,
        lax.all_gather(o_weight, "dp", axis=1, tiled=True),
        preferred_element_type=jnp.float32,
    )
    branch = lax.psum_scatter(projected, "image", scatter_dimension=1, tiled=True)
    mixed = jnp.tanh(gate[0]) * branch
    return mixed.astype(jnp.bfloat16)


def solution(mesh):
    in_specs = (
        P(("context", "dp"), "image"),
        P("image", ("context", "dp"), None),
        P(),
        P("dp", "image"),
        P("dp", "image"),
        P("dp", "image"),
        P("image", "dp"),
        P(),
        P(),
        P(),
        P(("context", "dp"), None),
        P(),
    )
    out_specs = P(("context", "dp"), "image")
    return jax.shard_map(local, mesh=mesh, in_specs=in_specs, out_specs=out_specs, check_vma=False)
```

profile of v0, /device:TPU:1, one launch (start us, length us, event | category | flops | bytes accessed | tf_op | source)
XLA Modules:
  0.0 868.0 jit_solution(17919678328717940517)
XLA Ops:
  10.0 39.6 %all-gather.15.cloned.1.call-done = bf16[8192,128]{1,0:T(8,128)(2,1)} async-done(((bf16[4096,128]{1,0:T(8,128)(2,1)}), bf16[8192,128]{1,0:T(8,128)(2,1)}) %all-gather.15.cloned.1.call-update) | async-done | bytes 2097168 | tf_op jit(solution)/shard_map/all_gather | solution.py:49
  49.6 49.1 %all-gather.13.cloned.1.call-done = bf16[8,32,8192]{2,1,0:T(8,128)(2,1)} async-done(((bf16[2,32,8192]{2,1,0:T(8,128)(2,1)}), bf16[8,32,8192]{2,1,0:T(8,128)(2,1)}) %all-gather.13.cloned.1.call-update) | async-done | bytes 4194320 | tf_op jit(solution)/shard_map/all_gather | solution.py:42
  98.7 4.2 multiply_reduce_fusion
  103.8 34.2 %all-gather.19.cloned.1.call-done = bf16[8192,128]{1,0:T(8,128)(2,1)} async-done(((bf16[4096,128]{1,0:T(8,128)(2,1)}), bf16[8192,128]{1,0:T(8,128)(2,1)}) %all-gather.19.cloned.1.call-update) | async-done | bytes 2097168 | tf_op jit(solution)/shard_map/all_gather | solution.py:50
  138.0 4.7 convolution_convert_fusion
  144.0 42.9 %all-gather.9.cloned.1.call-done = bf16[256,8192]{1,0:T(8,128)(2,1)} async-done(((bf16[256,2048]{1,0:T(8,128)(2,1)}), bf16[256,8192]{1,0:T(8,128)(2,1)}) %all-gather.9.cloned.1.call-update) | async-done | bytes 4194320 | tf_op jit(solution)/shard_map/all_gather | solution.py:31
  187.0 3.1 fusion.33
  190.1 201.9 %all-gather.11.cloned.1.call-done = bf16[8192,1024]{1,0:T(8,128)(2,1)} async-done(((bf16[4096,1024]{1,0:T(8,128)(2,1)}), bf16[8192,1024]{1,0:T(8,128)(2,1)}) %all-gather.11.cloned.1.call-update) | async-done | bytes 16777232 | tf_op jit(solution)/shard_map/all_gather | solution.py:37
  392.0 9.4 %fusion.36 = f32[256,1024]{1,0:T(8,128)S(1)} fusion(bf16[8192,1024]{1,0:T(8,128)(2,1)} %all-gather.11.cloned.1.call-done, bf16[256,8192]{1,0:T(8,128)(2,1)} %all-gather.9.cloned.1.call-done, f32[8192]{0:T(1024)S(1)} %copy-done.5, f32[256]{0:T(256)S(1)} %add_rsqrt_fusion.2), kind=kOutput, calls=%fused_computation.30 | convolution fusion | flops 4303355904 | bytes 22053888 | tf_op jit(solution)/shard_map/dot_general | solution.py:35
  402.7 73.5 %all-gather.17.cloned.1.call-done = bf16[8,1024,128]{2,1,0:T(8,128)(2,1)} async-done(((bf16[8,32,128]{2,1,0:T(8,128)(2,1)}), bf16[8,1024,128]{2,1,0:T(8,128)(2,1)}) %all-gather.17.cloned.1.call-update) | async-done | bytes 2097168 | tf_op jit(solution)/shard_map/all_gather | solution.py:75
  476.2 85.2 %all-gather.21.cloned.1.call-done = bf16[8,1024,128]{2,1,0:T(8,128)(2,1)} async-done(((bf16[8,32,128]{2,1,0:T(8,128)(2,1)}), bf16[8,1024,128]{2,1,0:T(8,128)(2,1)}) %all-gather.21.cloned.1.call-update) | async-done | bytes 2097168 | tf_op jit(solution)/shard_map/all_gather | solution.py:76
  561.3 65.1 %while.13 = (s32[]{:T(128)}, f32[8,1,256]{2,0,1:T(8,128)S(1)}, f32[8,1,256,128]{2,3,0,1:T(8,128)S(1)}, bf16[8,256,1,128]{3,1,2,0:T(8,128)(2,1)S(1)}, bf16[8,1024...) while((s32[]{:T(128)}, f32[8,1,256]{2,0,1:T(8,128)S(1)}, ...), condition=%wide.region_7.8_spmd.clone, body=%wide.region_4.7_spmd.clone.sunk | while | flops 1101038336 | bytes 38491284 | solution.py:102
  561.4 3.1 fusion.59
  564.6 2.4 fusion.60
  569.5 3.1 fusion.59
  572.6 2.4 fusion.60
  577.6 3.4 fusion.59
  581.0 2.4 fusion.60
  585.9 3.2 fusion.59
  589.2 2.4 fusion.60
  594.1 3.2 fusion.59
  597.3 2.4 fusion.60
  602.3 3.1 fusion.59
  605.4 2.4 fusion.60
  610.4 3.1 fusion.59
  613.5 2.4 fusion.60
  618.5 3.1 fusion.59
  621.6 2.4 fusion.60
  626.6 139.6 %all-gather.23.cloned.1.call-done = bf16[1024,8192]{1,0:T(8,128)(2,1)} async-done(((bf16[1024,4096]{1,0:T(8,128)(2,1)}), bf16[1024,8192]{1,0:T(8,128)(2,1)}) %all-gather.23.cloned.1.call-update) | async-done | bytes 16777232 | tf_op jit(solution)/shard_map/all_gather | solution.py:111
  766.1 12.7 %fusion.44 = f32[256,8192]{1,0:T(8,128)} fusion(bf16[256,1024]{0,1:T(8,128)(2,1)S(1)} %bitcast.82, bf16[1024,8192]{1,0:T(8,128)(2,1)} %all-gather.23.cloned.1.call-done), kind=kOutput, calls=%fused_computation.50 | convolution fusion | flops 4294967296 | bytes 25690112 | tf_op jit(solution)/shard_map/dot_general | solution.py:109
  779.6 79.2 %reduce-scatter.2.cloned.1.call-done = f32[256,2048]{1,0:T(8,128)} async-done(((f32[256,8192]{1,0:T(8,128)}), f32[256,2048]{1,0:T(8,128)}) %reduce-scatter.2.cloned.1.call-update) | async-done | bytes 2097168 | tf_op jit(solution)/shard_map/reduce_scatter | solution.py:114
  858.8 2.7 multiply_convert_fusion
  (117 shorter events, 26.6 us)
Async XLA Ops:
  6.5 43.0 %all-gather.15.cloned.1.call-start = ((), (), s32[]{:S(2)}) async-start(), calls=%async_computation.4 | async-start | bytes 3145728 | tf_op jit(solution)/shard_map/all_gather | solution.py:49
  7.3 91.4 %all-gather.13.cloned.1.call-start = ((), (), s32[]{:S(2)}) async-start(), calls=%async_computation.3 | async-start | bytes 5242880 | tf_op jit(solution)/shard_map/all_gather | solution.py:42
  8.0 95.0 %copy-start.1 = (f32[128]{0:T(128)S(1)}, f32[128]{0:T(128)}, u32[]{:S(2)}) copy-start(f32[128]{0:T(128)} %param.22) | copy-start | bytes 1540
  8.0 130.0 %all-gather.19.cloned.1.call-start = ((), (), s32[]{:S(2)}) async-start(), calls=%async_computation.6 | async-start | bytes 3145728 | tf_op jit(solution)/shard_map/all_gather | solution.py:50
  8.8 178.2 %all-gather.9.cloned.1.call-start = ((), (), s32[]{:S(2)}) async-start(), calls=%async_computation.1 | async-start | bytes 5242880 | tf_op jit(solution)/shard_map/all_gather | solution.py:31
  9.3 382.6 %all-gather.11.cloned.1.call-start = ((), (), s32[]{:S(2)}) async-start(), calls=%async_computation.2 | async-start | bytes 25165824 | tf_op jit(solution)/shard_map/all_gather | solution.py:37
  9.9 466.2 %all-gather.17.cloned.1.call-start = ((), (), s32[]{:S(2)}) async-start(), calls=%async_computation.5 | async-start | bytes 2162688 | tf_op jit(solution)/shard_map/all_gather | solution.py:75
  102.9 40.9 %copy-start.3 = (s32[8]{0:T(128)S(1)}, s32[8]{0:T(128)}, u32[]{:S(2)}) copy-start(s32[8]{0:T(128)} %param.25) | copy-start | bytes 100
  102.9 41.0 %copy-start = (s32[2,8]{1,0:T(2,128)S(1)}, s32[2,8]{1,0:T(2,128)}, u32[]{:S(2)}) copy-start(s32[2,8]{1,0:T(2,128)} %param.24) | copy-start | bytes 196
  103.7 288.2 %copy-start.5 = (f32[8192]{0:T(1024)S(1)}, f32[8192]{0:T(1024)}, u32[]{:S(2)}) copy-start(f32[8192]{0:T(1024)} %param.16) | copy-start | bytes 98308
  103.8 457.6 %all-gather.21.cloned.1.call-start = ((), (), s32[]{:S(2)}) async-start(), calls=%async_computation.7 | async-start | bytes 2162688 | tf_op jit(solution)/shard_map/all_gather | solution.py:76
  142.8 623.3 %all-gather.23.cloned.1.call-start = ((), (), s32[]{:S(2)}) async-start(), calls=%async_computation.8 | async-start | bytes 25165824 | tf_op jit(solution)/shard_map/all_gather | solution.py:111
  143.6 715.2 %reduce-scatter.2.cloned.1.call-start = ((), (), s32[]{:S(2)}) async-start(), calls=%async_computation.9 | async-start | bytes 10485760 | tf_op jit(solution)/shard_map/reduce_scatter | solution.py:114
  190.1 212.2 %copy-start.2 = (f32[128]{0:T(128)S(1)}, f32[128]{0:T(128)}, u32[]{:S(2)}) copy-start(f32[128]{0:T(128)} %param.21) | copy-start | bytes 1540
  561.4 5.6 copy-start.4
  569.5 5.6 copy-start.4
  577.6 5.8 copy-start.4
  585.9 5.7 copy-start.4
  594.1 5.7 copy-start.4
  602.3 5.6 copy-start.4
  610.4 5.6 copy-start.4
  618.5 5.6 copy-start.4
Sparse Core Ops, SparseCore 0:
  9.0 40.5 all-gather.14
  51.2 47.4 all-gather.12
  100.3 37.6 all-gather.18
  139.6 47.3 all-gather.8
  188.5 203.4 all-gather.10
  393.5 82.6 all-gather.16
  477.8 83.4 all-gather.20
  563.0 203.0 all-gather.22
  779.0 79.7 reduce-scatter.1
where the time goes:
time: 868 us
  waiting for transfers between devices  749 us (86%)
  matrix products  74.3 us (9%)
  other arithmetic  27.1 us (3%)
  between operations  14 us (2%)
    all_gather x1, waiting for transfers between devices, local(): lax.all_gather(q_weight, 'dp', axis=0, tiled=True)  202 us
    all_gather x1, waiting for transfers between devices, local(): lax.all_gather(o_weight, 'dp', axis=1, tiled=True)  140 us
    all_gather x1, waiting for transfers between devices, local(): lax.all_gather(values, ('context', 'dp'), axis=1, tiled=True)  85.2 us
    reduce_scatter x1, waiting for transfers between devices, local(): lax.psum_scatter(projected, 'image', scatter_dimension=1, tiled=True)  79.2 us
    all_gather x1, waiting for transfers between devices, local(): lax.all_gather(keys, ('context', 'dp'), axis=1, tiled=True)  73.5 us
    all_gather x1, waiting for transfers between devices, local(): all_patches = lax.all_gather(patches, 'image', axis=0, tiled=True)  49.1 us
    all_gather x1, waiting for transfers between devices, local(): whole = lax.all_gather(text, 'image', axis=1, tiled=True)  42.9 us
    all_gather x1, waiting for transfers between devices, local(): lax.all_gather(k_weight, 'dp', axis=0, tiled=True)  39.6 us
  transfers between devices with their start and end apart: 9, of which 9 were waited for; matrix products, arithmetic and copies ran while one was open for 10% of the time, Pallas kernels for 0%

commit v1 on v0

v1 whole, which is shorter than its diff:
```python
import functools

import jax
import jax.numpy as jnp
from jax import lax
from jax.experimental import pallas as pl
from jax.experimental.pallas import tpu as pltpu
from jax.sharding import PartitionSpec as P

MESH = pl.DeviceIdType.MESH
BF16 = jnp.bfloat16
F32 = jnp.float32
ANY = pl.BlockSpec(memory_space=pl.ANY)
VMEM = pl.BlockSpec(memory_space=pltpu.VMEM)
D = 8192
HD = 128
BLOCK = 128
EPS = 1e-05
NQ = 4


def place():
    x = lax.axis_index("image")
    ctx = lax.axis_index("context")
    zh = lax.axis_index("dp")
    return x, ctx // 4, zh, (ctx // 2) % 2, ctx % 2


def send(src, dst, ss, rs, dev):
    return pltpu.make_async_remote_copy(
        src_ref=src, dst_ref=dst, send_sem=ss, recv_sem=rs, device_id=dev, device_id_type=MESH
    )


def rms(v, gain):
    ms = jnp.mean(v * v, axis=-1, keepdims=True)
    return v * lax.rsqrt(ms + EPS) * gain


def gather_kernel(
    text, patches, gain, qw, kw, vw, ow, qg, kg,
    q_out, kv, wo,
    raw, tn, pb, wq, wkv, acc, kvacc, kvown, sums,
    loc, sum_s, sum_r, ps, pr, ts, tr, ks, kr, qs, qr, os, orr, gs, gr, hs, hr,
):
    x, y, zh, zl, c = place()
    ctx = lax.axis_index("context")
    z = zh * 2 + zl
    xr, xl, xo = (x + 1) % 4, (x + 3) % 4, (x + 2) % 4
    right, left = {"image": xr}, {"image": xl}
    sib = {"context": ctx + 1 - 2 * c}
    near = {"context": ctx + 2 - 4 * zl}
    cross = {"context": ctx + 2 - 4 * zl, "dp": 1 - zh}
    yr = {"context": ((y + 1) % 4) * 4 + zl * 2 + c}
    yl = {"context": ((y + 3) % 4) * 4 + zl * 2 + c}

    def plane(k, sign):
        ty = (y + sign * (k // 4) + 4) % 4
        tz = (z + sign * (k % 4) + 4) % 4
        return ty * 4 + (tz % 2) * 2 + c, tz // 2

    barrier = pltpu.get_barrier_semaphore()
    for d in (1, 2, 3):
        pl.semaphore_signal(barrier, inc=1, device_id={"image": (x + d) % 4}, device_id_type=MESH)
    pl.semaphore_signal(barrier, inc=1, device_id=sib, device_id_type=MESH)

    def greet(k, carry):
        tc, td = plane(k, 1)
        pl.semaphore_signal(barrier, inc=1, device_id={"context": tc, "dp": td}, device_id_type=MESH)
        return carry

    lax.fori_loop(1, 16, greet, 0)

    own_half = pl.ds(zh * 4096, 4096)
    local = [
        pltpu.make_async_copy(text, raw, loc.at[0]),
        pltpu.make_async_copy(patches, pb.at[pl.ds(x * 64, 64)], loc.at[1]),
        pltpu.make_async_copy(kw, wkv.at[own_half, pl.ds(0, 128)], loc.at[2]),
        pltpu.make_async_copy(vw, wkv.at[own_half, pl.ds(128, 128)], loc.at[3]),
        pltpu.make_async_copy(qw, wq.at[own_half], loc.at[4]),
        pltpu.make_async_copy(ow, wo.at[:, own_half], loc.at[5]),
    ]
    for cp in local:
        cp.start()
    pl.semaphore_wait(barrier, 19)
    sends = []

    def go(cp):
        cp.start()
        sends.append(cp)
        return cp

    def prow(slot, half):
        return pb.at[pl.ds(slot * 64 + half * 32, 32)]

    p_r = [go(send(patches.at[pl.ds(0, 32)], prow(x, 0), ps.at[0], pr.at[0], right))]
    p_l = [go(send(patches.at[pl.ds(32, 32)], prow(x, 1), ps.at[3], pr.at[3], left))]

    other = (1 - zh) * 4096

    def kv_flow(base, a, b, dev):
        rows = pl.ds(base + a * 2048 + b * 1024, 1024)
        return rows

    rows_mine = pl.ds(c * 2048 + zl * 1024, 1024)
    rows_there = pl.ds(zh * 4096 + c * 2048 + zl * 1024, 1024)
    k1 = [
        go(send(kw.at[rows_mine], wkv.at[rows_there, pl.ds(0, 128)], ks.at[0], kr.at[0], cross)),
        go(send(vw.at[rows_mine], wkv.at[rows_there, pl.ds(128, 128)], ks.at[1], kr.at[1], cross)),
    ]
    p_r.append(go(send(patches.at[pl.ds(32, 32)], prow(x, 1), ps.at[1], pr.at[1], right)))
    p_l.append(go(send(patches.at[pl.ds(0, 32)], prow(x, 0), ps.at[4], pr.at[4], left)))

    def orow(cy, p):
        return pl.ds(c * 512 + ((cy + 4) % 4) * 128 + p * 64, 64)

    ocol = pl.ds((1 - zh) * 4096, 4096)
    o1 = go(send(ow.at[orow(y, zl)], wo.at[orow(y, zl), own_half], os.at[0], orr.at[0], cross))

    def wq_rows(h, cc, p, j):
        return pl.ds(h * 4096 + cc * 2048 + p * 1024 + j * (1024 // NQ), 1024 // NQ)

    q1 = [
        go(send(qw.at[wq_rows(0, c, zl, j)], wq.at[wq_rows(zh, c, zl, j)], qs.at[0, j], qr.at[0, j], cross))
        for j in range(NQ)
    ]

    local[0].wait()
    part = jnp.zeros((256, 128), F32)
    for j in range(16):
        t = raw[:, j * 128 : (j + 1) * 128].astype(F32)
        part = part + t * t
    row = jnp.sum(part.T, axis=0, keepdims=True)
    sums[x] = jnp.broadcast_to(row, (8, 256))
    s_cp = [
        go(send(sums.at[x], sums.at[x], sum_s.at[d - 1], sum_r.at[d - 1], {"image": (x + d) % 4}))
        for d in (1, 2, 3)
    ]
    for cp in s_cp:
        cp.wait_recv()
    total = sums[0] + sums[1] + sums[2] + sums[3]
    inv = lax.rsqrt(total[0:1] * (1.0 / D) + EPS)
    inv = jnp.broadcast_to(inv, (128, 256)).T
    for j in range(16):
        t = raw[:, j * 128 : (j + 1) * 128].astype(F32)
        g = gain[pl.ds(x * 16 + j, 1), :]
        tn[x, :, j * 128 : (j + 1) * 128] = (t * inv * g).astype(BF16)

    p_r[0].wait_recv()
    p_r.append(go(send(prow(xl, 0), prow(xl, 0), ps.at[2], pr.at[2], right)))
    p_l[0].wait_recv()
    p_l.append(go(send(prow(xr, 1), prow(xr, 1), ps.at[5], pr.at[5], left)))

    def wkv_at(cc, p, v):
        return wkv.at[pl.ds(other + cc * 2048 + p * 1024, 1024), pl.ds(v * 128, 128)]

    k2, k3 = [], []
    for v in (0, 1):
        k1[v].wait_recv()
        piece = wkv_at(c, 1 - zl, v)
        k2.append(go(send(piece, piece, ks.at[2 + v], kr.at[2 + v], near)))
        k3.append(go(send(piece, piece, ks.at[4 + v], kr.at[4 + v], sib)))

    p_r[1].wait_recv()
    p_l[1].wait_recv()

    def trow(slot, half):
        return tn.at[slot, pl.ds(half * 128, 128)]

    t_r = [go(send(trow(x, 0), trow(x, 0), ts.at[0], tr.at[0], right))]
    t_l = [go(send(trow(x, 1), trow(x, 1), ts.at[3], tr.at[3], left))]
    t_r.append(go(send(trow(x, 1), trow(x, 1), ts.at[1], tr.at[1], right)))
    t_l.append(go(send(trow(x, 0), trow(x, 0), ts.at[4], tr.at[4], left)))

    for v in (0, 1):
        k2[v].wait_recv()
        piece = wkv_at(c, zl, v)
        k3.append(go(send(piece, piece, ks.at[6 + v], kr.at[6 + v], sib)))

    o1.wait_recv()

    def opiece(cy, p):
        return wo.at[orow(cy, p), ocol]

    osib = []

    def oto(cy, p, idx, dev):
        piece = opiece(cy, p)
        return go(send(piece, piece, os.at[idx], orr.at[idx], dev))

    o2 = oto(y, 1 - zl, 1, near)
    o_r = [oto(y, 1 - zl, 2, yr)]
    o_l = [oto(y, 1 - zl, 5, yl)]
    osib.append(oto(y, 1 - zl, 8, sib))

    q2, q3 = [], []

    def q_pass(j):
        q1[j].wait_recv()
        piece = wq.at[wq_rows(1 - zh, c, 1 - zl, j)]
        q2.append(go(send(piece, piece, qs.at[1, j], qr.at[1, j], near)))
        q3.append(go(send(piece, piece, qs.at[2, j], qr.at[2, j], sib)))

    def q_last(j):
        q2[j].wait_recv()
        piece = wq.at[wq_rows(1 - zh, c, zl, j)]
        q3.append(go(send(piece, piece, qs.at[3, j], qr.at[3, j], sib)))

    q_pass(0)

    p_r[2].wait_recv()
    p_l[2].wait_recv()
    for i in (1, 2, 3):
        local[i].wait()
    for cp in k3:
        cp.wait_recv()
    kvacc[...] = jnp.zeros_like(kvacc)

    def kv_step(i, carry):
        cols = pl.ds(pl.multiple_of(i * 1024, 1024), 1024)
        kvacc[...] += jnp.dot(pb[:, cols], wkv[cols, :], preferred_element_type=F32)
        return carry

    lax.fori_loop(0, 8, kv_step, 0)
    keys = rms(kvacc[:, 0:128], kg[...]).astype(BF16)
    kvown[:, :, 0:128] = keys.reshape(8, 32, 128)
    kvown[:, :, 128:256] = kvacc[:, 128:256].astype(BF16).reshape(8, 32, 128)

    def kv_at(cc, d):
        return kv.at[:, pl.ds((cc * 2 + d) * 32, 32), :]

    def kv_send(k):
        tc, td = plane(k, 1)
        return send(kvown, kv_at(ctx, zh), gs.at[k], gr.at[k], {"context": tc, "dp": td})

    def kv_start(k, carry):
        kv_send(k).start()
        return carry

    lax.fori_loop(1, 16, kv_start, 0)
    go(send(kvown, kv_at(ctx, zh), hs.at[0], hr.at[0], sib))
    keep = pltpu.make_async_copy(kvown, kv_at(ctx, zh), loc.at[6])
    keep.start()

    o2.wait_recv()
    o_r.append(oto(y, zl, 3, yr))
    o_l.append(oto(y, zl, 6, yl))
    osib.append(oto(y, zl, 9, sib))
    q_pass(1)
    q_last(0)

    t_r[0].wait_recv()
    t_r.append(go(send(trow(xl, 0), trow(xl, 0), ts.at[2], tr.at[2], right)))
    t_l[0].wait_recv()
    t_l.append(go(send(trow(xr, 1), trow(xr, 1), ts.at[5], tr.at[5], left)))

    o_r[0].wait_recv()
    o_r.append(oto(y - 1, 1 - zl, 4, yr))
    osib.append(oto(y - 1, 1 - zl, 10, sib))
    o_l[0].wait_recv()
    osib.append(oto(y + 1, 1 - zl, 11, sib))
    q_pass(2)
    q_last(1)
    o_r[1].wait_recv()
    osib.append(oto(y - 1, zl, 12, sib))
    o_l[1].wait_recv()
    o_l.append(oto(y + 1, zl, 7, yl))
    osib.append(oto(y + 1, zl, 13, sib))
    q_pass(3)
    q_last(2)

    def kv_pass(k, carry):
        kv_send(k).wait_recv()
        sc, sd = plane(k, -1)
        send(kv_at(sc, sd), kv_at(sc, sd), hs.at[k], hr.at[k], sib).start()
        return carry

    lax.fori_loop(1, 16, kv_pass, 0)
    q_last(3)
    o_r[2].wait_recv()
    osib.append(oto(y - 2, 1 - zl, 14, sib))
    o_l[2].wait_recv()
    osib.append(oto(y + 2, zl, 15, sib))

    local[4].wait()
    for cp in q3:
        cp.wait_recv()

    def project(slot):
        def step(i, carry):
            cols = pl.ds(pl.multiple_of(i * 512, 512), 512)
            rows = pl.ds(pl.multiple_of(slot * 2048 + i * 512, 512), 512)
            acc[...] += jnp.dot(tn[slot, :, cols], wq[rows, :], preferred_element_type=F32)
            return carry

        lax.fori_loop(0, 4, step, 0)

    acc[...] = jnp.zeros_like(acc)
    project(x)
    t_r[1].wait_recv()
    project(xl)
    t_l[1].wait_recv()
    project(xr)
    t_r[2].wait_recv()
    t_l[2].wait_recv()
    project(xo)
    for h in range(8):
        q_out[:, h * HD : (h + 1) * HD] = rms(acc[:, h * HD : (h + 1) * HD], qg[...]).astype(BF16)

    local[5].wait()
    keep.wait()

    def kv_end(k, carry):
        kv_send(k).wait_send()
        return carry

    lax.fori_loop(1, 16, kv_end, 0)

    def sib_end(k, carry):
        sc, sd = plane(k, -1)
        cp = send(kv_at(sc, sd), kv_at(sc, sd), hs.at[k], hr.at[k], sib)
        cp.wait_recv()
        cp.wait_send()
        return carry

    lax.fori_loop(1, 16, sib_end, 0)
    send(kvown, kv_at(ctx, zh), hs.at[0], hr.at[0], sib).wait_recv()
    for cp in osib:
        cp.wait_recv()
    for cp in sends:
        cp.wait_send()


def gather_call(text, patches, in_gain, qw, kw, vw, ow, q_gain, k_gain):
    dma = pltpu.SemaphoreType.DMA
    return pl.pallas_call(
        gather_kernel,
        name="gather_project",
        out_shape=(
            jax.ShapeDtypeStruct((256, 1024), BF16),
            jax.ShapeDtypeStruct((8, 1024, 256), BF16),
            jax.ShapeDtypeStruct((1024, D), BF16),
        ),
        in_specs=[ANY, ANY, VMEM, ANY, ANY, ANY, ANY, VMEM, VMEM],
        out_specs=(VMEM, ANY, ANY),
        scratch_shapes=[
            pltpu.VMEM((256, 2048), BF16),
            pltpu.VMEM((4, 256, 2048), BF16),
            pltpu.VMEM((256, D), BF16),
            pltpu.VMEM((D, 1024), BF16),
            pltpu.VMEM((D, 256), BF16),
            pltpu.VMEM((256, 1024), F32),
            pltpu.VMEM((256, 256), F32),
            pltpu.VMEM((8, 32, 256), BF16),
            pltpu.VMEM((4, 8, 256), F32),
            dma((7,)), dma((3,)), dma((3,)), dma((6,)), dma((6,)), dma((6,)), dma((6,)),
            dma((8,)), dma((8,)), dma((4, NQ)), dma((4, NQ)), dma((16,)), dma((16,)),
            dma((16,)), dma((16,)), dma((16,)), dma((16,)),
        ],
        compiler_params=pltpu.CompilerParams(
            collective_id=0, has_side_effects=True, vmem_limit_bytes=56 << 20
        ),
    )(
        text, patches.reshape(64, D), in_gain.reshape(64, 128), qw, kw, vw, ow,
        q_gain.reshape(1, HD), k_gain.reshape(1, HD),
    )


LOG2E = 1.4426950408889634


def attend_kernel(mask, owner, q, kv, out, qh, m, l, a):
    s = pl.program_id(0)
    image = owner[s]

    @pl.when(s == 0)
    def _():
        m[...] = jnp.full_like(m, -1e30)
        l[...] = jnp.zeros_like(l)
        a[...] = jnp.zeros_like(a)
        for b in range(2):
            for h in range(8):
                qh[b, h * 128 : (h + 1) * 128, :] = q[b * 128 : (b + 1) * 128, h * 128 : (h + 1) * 128]

    scale = LOG2E / HD**0.5
    for b in range(2):

        @pl.when(mask[b, image] > 0)
        def _(b=b):
            keys = kv[0, :, 0:128]
            vals = kv[0, :, 128:256]
            for t in range(4):
                rows = slice(t * 256, (t + 1) * 256)
                sc = lax.dot_general(
                    qh[b, rows, :], keys, (((1,), (1,)), ((), ())), preferred_element_type=F32
                )
                old = m[b, rows, :]
                new = jnp.maximum(old, jnp.max(sc, axis=-1, keepdims=True) * scale)
                w = jnp.exp2(sc * scale - new[:, 0:1])
                fac = jnp.exp2(old - new)
                l[b, rows, :] = l[b, rows, :] * fac + jnp.sum(w, axis=-1, keepdims=True)
                a[b, rows, :] = a[b, rows, :] * fac + jnp.dot(
                    w.astype(BF16), vals, preferred_element_type=F32
                )
                m[b, rows, :] = new

    @pl.when(s == 7)
    def _():
        for b in range(2):
            for h in range(8):
                rows = slice(h * 128, (h + 1) * 128)
                out[b * 128 : (b + 1) * 128, rows] = (a[b, rows, :] / l[b, rows, :]).astype(BF16)


def attend_call(q, kv, mask, owner):
    return pl.pallas_call(
        attend_kernel,
        name="attend",
        out_shape=jax.ShapeDtypeStruct((256, 1024), BF16),
        grid_spec=pltpu.PrefetchScalarGridSpec(
            num_scalar_prefetch=2,
            grid=(8,),
            in_specs=[
                pl.BlockSpec((256, 1024), lambda s, *_: (0, 0)),
                pl.BlockSpec((1, 1024, 256), lambda s, *_: (s, 0, 0)),
            ],
            out_specs=pl.BlockSpec((256, 1024), lambda s, *_: (0, 0)),
            scratch_shapes=[
                pltpu.VMEM((2, 1024, 128), BF16),
                pltpu.VMEM((2, 1024, 128), F32),
                pltpu.VMEM((2, 1024, 128), F32),
                pltpu.VMEM((2, 1024, 128), F32),
            ],
        ),
        compiler_params=pltpu.CompilerParams(vmem_limit_bytes=48 << 20),
    )(mask, owner, q, kv)


def output_kernel(att, wo, gate, out, w, part, give, take, loc, ss, rs):
    x = lax.axis_index("image")
    xr, xl, xo = (x + 1) % 4, (x + 3) % 4, (x + 2) % 4
    right, left = {"image": xr}, {"image": xl}
    order = (xo, xr, xl, x)
    cps = [
        pltpu.make_async_copy(wo.at[:, pl.ds(t * 2048, 2048)], w.at[i], loc.at[i])
        for i, t in enumerate(order)
    ]
    for cp in cps:
        cp.start()
    barrier = pltpu.get_barrier_semaphore()
    for dev in (right, left):
        pl.semaphore_signal(barrier, inc=1, device_id=dev, device_id_type=MESH)
    pl.semaphore_wait(barrier, 2)

    def product(i, store):
        cps[i].wait()

        def step(n, carry):
            cols = pl.ds(pl.multiple_of(n * 512, 512), 512)
            store(cols, jnp.dot(att[...], w[i, :, cols], preferred_element_type=F32))
            return carry

        lax.fori_loop(0, 4, step, 0)

    def copy(i, dev):
        return send(give.at[i], take.at[i], ss.at[i], rs.at[i], dev)

    def far(cols, v):
        give[0, :, cols] = v[0:128].astype(BF16)
        give[1, :, cols] = v[128:256].astype(BF16)

    product(0, far)
    c0, c1 = copy(0, right), copy(1, left)
    c0.start()
    c1.start()

    def to_right(cols, v):
        give[3, :, cols] = v[128:256].astype(BF16)
        part[0, :, cols] = v[0:128]

    product(1, to_right)
    c3 = copy(3, right)
    c3.start()

    def to_left(cols, v):
        give[4, :, cols] = v[0:128].astype(BF16)
        part[1, :, cols] = v[128:256]

    product(2, to_left)
    c4 = copy(4, left)
    c4.start()

    c0.wait_recv()
    give[2] = (part[0] + take[0].astype(F32)).astype(BF16)
    c2 = copy(2, right)
    c2.start()
    c1.wait_recv()
    give[5] = (part[1] + take[1].astype(F32)).astype(BF16)
    c5 = copy(5, left)
    c5.start()

    def mine(cols, v):
        part[0, :, cols] = v[0:128]
        part[1, :, cols] = v[128:256]

    product(3, mine)
    scale = jnp.tanh(jnp.full((8, 128), gate[0], F32))[0:1, 0:1]
    c3.wait_recv()
    c4.wait_recv()
    c2.wait_recv()
    out[0:128] = (scale * (part[0] + take[2].astype(F32) + take[4].astype(F32))).astype(BF16)
    c5.wait_recv()
    out[128:256] = (scale * (part[1] + take[3].astype(F32) + take[5].astype(F32))).astype(BF16)
    for cp in (c0, c1, c2, c3, c4, c5):
        cp.wait_send()


def output_call(att, wo, gate):
    dma = pltpu.SemaphoreType.DMA
    return pl.pallas_call(
        output_kernel,
        name="output",
        out_shape=jax.ShapeDtypeStruct((256, 2048), BF16),
        in_specs=[VMEM, ANY, pl.BlockSpec(memory_space=pltpu.SMEM)],
        out_specs=VMEM,
        scratch_shapes=[
            pltpu.VMEM((4, 1024, 2048), BF16),
            pltpu.VMEM((2, 128, 2048), F32),
            pltpu.VMEM((6, 128, 2048), BF16),
            pltpu.VMEM((6, 128, 2048), BF16),
            dma((4,)), dma((6,)), dma((6,)),
        ],
        compiler_params=pltpu.CompilerParams(
            collective_id=1, has_side_effects=True, vmem_limit_bytes=48 << 20
        ),
    )(att, wo, gate)


def local(
    text, patches, in_gain, q_weight, k_weight, v_weight, o_weight, q_gain, k_gain, gate, block_mask, owner_ids
):
    q, kv, wo = gather_call(
        text, patches, in_gain, q_weight, k_weight, v_weight, o_weight, q_gain, k_gain
    )
    att = attend_call(q, kv, block_mask, owner_ids)
    return output_call(att, wo, gate)


def solution(mesh):
    in_specs = (
        P(("context", "dp"), "image"),
        P("image", ("context", "dp"), None),
        P(),
        P("dp", "image"),
        P("dp", "image"),
        P("dp", "image"),
        P("image", "dp"),
        P(),
        P(),
        P(),
        P(("context", "dp"), None),
        P(),
    )
    out_specs = P(("context", "dp"), "image")
    return jax.shard_map(local, mesh=mesh, in_specs=in_specs, out_specs=out_specs, check_vma=False)
```

time: 868 us -> 329 us (0.38)
  waiting for transfers between devices: 749 us -> 0 us
  Pallas kernels: 0 us -> 318 us
  matrix products: 74.3 us -> 0 us
  other arithmetic: 27.1 us -> 0 us
  between operations: 14 us -> 0.7 us
    all_gather x8 -> x0, waiting for transfers between devices: 666 us -> none  [the longest x1 202 us: local(): lax.all_gather(q_weight, 'dp', axis=0, tiled=True)]
    pallas_call x0 -> x3, Pallas kernels: none -> 318 us  [the longest x1 259 us: gather_call(): pl.pallas_call(gather_kernel, name='gather_project', out_shape=(jax.Shape...]
    reduce_scatter x1 -> x0, waiting for transfers between devices: 79.2 us -> none  [local(): lax.psum_scatter(projected, 'image', scatter_dimension=1, tiled=True)]
    dot_general x20 -> x0, matrix products: 74.3 us -> none  [the longest x8 25.4 us: one_group(): jnp.einsum('tjd,irjd->jtir', group_queries, key_piece, preferred_element_...]
    reduce_sum x11 -> x0, other arithmetic: 22.9 us -> none  [the longest x8 19.4 us: one_group(): new_total = running_total * factor + jnp.sum(weights, axis=(2, 3))]
  transfers between devices with their start and end apart: 9 -> 0, of which waited for: 9 -> 0; matrix products, arithmetic and copies ran while one was open for 10% -> 0% of each run, Pallas kernels for 0% -> 0%
where the time goes in v1:
time: 329 us; the launch traced here: 323 us
  Pallas kernels  318 us (97%)
  local copies, waits for them, and re-layouts  4.2 us (1%)
    pallas_call x1, Pallas kernels, gather_call(): pl.pallas_call(gather_kernel, name='gather_project', out_shape=(jax.Shape...  259 us
    pallas_call x1, Pallas kernels, output_call(): pl.pallas_call(output_kernel, name='output', out_shape=jax.ShapeDtypeStru...  35.9 us
    pallas_call x1, Pallas kernels, attend_call(): pl.pallas_call(attend_kernel, name='attend', out_shape=jax.ShapeDtypeStru...  23.6 us

profile of v1, /device:TPU:1, one launch (start us, length us, event | category | flops | bytes accessed | tf_op | source)
XLA Modules:
  0.0 323.2 jit_solution(7467036496752347341)
XLA Ops:
  0.0 0.0 copy-start.2
  0.0 0.0 copy-start.3
  0.0 258.8 %gather_project.1 = (bf16[256,1024]{1,0:T(8,128)(2,1)}, bf16[8,1024,256]{2,1,0:T(8,128)(2,1)}, bf16[1024,8192]{1,0:T(8,128)(2,1)}) custom-call(bf16[256,2048]{1,0:T(8,128)(2,1)} %text.1, bf16[64,8192]{1,0:T(8,128)(2,1)} %bitcast.4, f32[64,128]{1,0:T(8,128)} %bitcast.5, bf16[4096,1024]{1,0:T(8,128)(2,1)} %qw.1, bf16[4096,128]{1,0:T(8,128)(2,1)} %kw.1, ...), custom_call_target="tpu_custom_call" | custom-call | tf_op jit(solution)/shard_map/gather_project/pallas_call | solution.py:336
  258.8 0.0 copy-done.2
  258.8 0.0 copy-done.3
  258.9 0.0 copy-start
  258.9 2.2 copy-done
  261.0 0.0 copy-start.1
  261.0 1.0 copy-done.1
  262.1 23.6 %attend.1.att = bf16[256,1024]{1,0:T(8,128)(2,1)S(1)} custom-call(s32[2,8]{1,0:T(2,128)S(1)} %copy-done.2, s32[8]{0:T(128)S(1)} %copy-done.3, bf16[256,1024]{1,0:T(8,128)(2,1)S(1)} %copy-done.1, bf16[8,1024,256]{2,1,0:T(8,128)(2,1)S(1)} %copy-done), custom_call_target="tpu_custom_call" | custom-call | tf_op jit(solution)/shard_map/attend/pallas_call | solution.py:416
  286.3 35.9 %output.1 = bf16[256,2048]{1,0:T(8,128)(2,1)S(1)} custom-call(bf16[256,1024]{1,0:T(8,128)(2,1)S(1)} %attend.1.att, bf16[1024,8192]{1,0:T(8,128)(2,1)} %get-tuple-element.10.wo, f32[1]{0:T(128)S(6)} %copy.14.gate), custom_call_target="tpu_custom_call" | custom-call | tf_op jit(solution)/shard_map/output/pallas_call | solution.py:520
  322.2 1.0 copy.15
Async XLA Ops:
  0.0 258.8 %copy-start.2 = (s32[2,8]{1,0:T(2,128)S(1)}, s32[2,8]{1,0:T(2,128)}, u32[]{:S(2)}) copy-start(s32[2,8]{1,0:T(2,128)} %mask.1) | copy-start | bytes 196
  0.0 258.8 %copy-start.3 = (s32[8]{0:T(128)S(1)}, s32[8]{0:T(128)}, u32[]{:S(2)}) copy-start(s32[8]{0:T(128)} %owner.1) | copy-start | bytes 100
  258.9 2.2 copy-start
  261.0 1.0 copy-start.1

commit v2 on v0

v2 whole, which is shorter than its diff:
```python
import jax
import jax.numpy as jnp
from jax import lax
from jax.experimental import pallas as pl
from jax.experimental.pallas import tpu as pltpu
from jax.sharding import PartitionSpec as P

MESH = pl.DeviceIdType.MESH
BF16 = jnp.bfloat16
F32 = jnp.float32
ANY = pl.BlockSpec(memory_space=pl.ANY)
VMEM = pl.BlockSpec(memory_space=pltpu.VMEM)
D = 8192
HD = 128
BLOCK = 128
EPS = 1e-05
NQ = 4
HALF = 64
LOG2E = 1.4426950408889634
SCALE = LOG2E / HD**0.5


def place():
    x = lax.axis_index("image")
    ctx = lax.axis_index("context")
    zh = lax.axis_index("dp")
    return x, ctx // 4, zh, (ctx // 2) % 2, ctx % 2


def send(src, dst, ss, rs, dev):
    return pltpu.make_async_remote_copy(
        src_ref=src, dst_ref=dst, send_sem=ss, recv_sem=rs, device_id=dev, device_id_type=MESH
    )


def rms(v, gain):
    ms = jnp.mean(v * v, axis=-1, keepdims=True)
    return v * lax.rsqrt(ms + EPS) * gain


def kernel(
    text, patches, gain, qw, kw, vw, ow, qg, kg, gate, mask, owner,
    out, wo,
    raw, tn, pb, wq, wkv, acc, kvacc, kvb, sums, qh, m, l, a, att, part, give, take,
    loc, wload, sum_s, sum_r, ps, pr, ts, tr, ks, kr, qs, qr, os, orr, gs, gr, hs, hr, rs, rr,
):
    x, y, zh, zl, c = place()
    ctx = lax.axis_index("context")
    z = zh * 2 + zl
    xr, xl, xo = (x + 1) % 4, (x + 3) % 4, (x + 2) % 4
    right, left = {"image": xr}, {"image": xl}
    sib = {"context": ctx + 1 - 2 * c}
    near = {"context": ctx + 2 - 4 * zl}
    cross = {"context": ctx + 2 - 4 * zl, "dp": 1 - zh}

    def at(dy, dz):
        tz = (z + dz + 4) % 4
        return ((y + dy + 4) % 4) * 4 + (tz % 2) * 2 + c, tz // 2

    def to(dy, dz):
        tc, td = at(dy, dz)
        return {"context": tc, "dp": td}

    yr, yl = to(1, 0), to(3, 0)
    barrier = pltpu.get_barrier_semaphore()
    greeted = [{"image": (x + d) % 4} for d in (1, 2, 3)] + [to(d, 0) for d in (1, 2, 3)]
    greeted += [to(0, d) for d in (1, 2, 3)] + [sib]
    for dev in greeted:
        pl.semaphore_signal(barrier, inc=1, device_id=dev, device_id_type=MESH)

    own_half = pl.ds(zh * 4096, 4096)
    local = [
        pltpu.make_async_copy(text, raw, loc.at[0]),
        pltpu.make_async_copy(patches, pb.at[pl.ds(x * 64, 64)], loc.at[1]),
        pltpu.make_async_copy(kw, wkv.at[own_half, pl.ds(0, 128)], loc.at[2]),
        pltpu.make_async_copy(vw, wkv.at[own_half, pl.ds(128, 128)], loc.at[3]),
        pltpu.make_async_copy(qw, wq.at[pl.ds(zh * 4, 4)], loc.at[4]),
    ]
    for cp in local:
        cp.start()
    pl.semaphore_wait(barrier, len(greeted))
    sends = []

    def go(cp):
        cp.start()
        sends.append(cp)
        return cp

    def prow(slot, i):
        return pb.at[pl.ds(slot * 64 + i * 16, 16)]

    def p_first(n):
        p_r.append(go(send(patches.at[pl.ds(n * 16, 16)], prow(x, n), ps.at[n], pr.at[n], right)))
        i = 3 - n
        p_l.append(go(send(patches.at[pl.ds(i * 16, 16)], prow(x, i), ps.at[6 + n], pr.at[6 + n], left)))

    p_r, p_l = [], []
    p_first(0)

    rows_mine = pl.ds(c * 2048 + zl * 1024, 1024)
    rows_there = pl.ds(zh * 4096 + c * 2048 + zl * 1024, 1024)
    k1 = [
        go(send(kw.at[rows_mine], wkv.at[rows_there, pl.ds(0, 128)], ks.at[0], kr.at[0], cross)),
        go(send(vw.at[rows_mine], wkv.at[rows_there, pl.ds(128, 128)], ks.at[1], kr.at[1], cross)),
    ]
    for n in (1, 2, 3):
        p_first(n)

    def orow(cy, p):
        return pl.ds(c * 512 + ((cy + 4) % 4) * 128 + p * 64, 64)

    o1 = go(send(ow.at[orow(y, zl)], wo.at[orow(y, zl)], os.at[0], orr.at[0], cross))

    rows_q = 1024 // NQ

    def wq_at(h, cc, p, j):
        return wq.at[h * 4 + cc * 2 + p, pl.ds(j * rows_q, rows_q)]

    q1 = [
        go(send(qw.at[c * 2 + zl, pl.ds(j * rows_q, rows_q)], wq_at(zh, c, zl, j), qs.at[0, j], qr.at[0, j], cross))
        for j in range(NQ)
    ]

    local[0].wait()
    lanes = jnp.zeros((256, 128), F32)
    for j in range(16):
        t = raw[:, j * 128 : (j + 1) * 128].astype(F32)
        lanes = lanes + t * t
    row = jnp.sum(lanes.T, axis=0, keepdims=True)
    sums[x] = jnp.broadcast_to(row, (8, 256))
    s_cp = [
        go(send(sums.at[x], sums.at[x], sum_s.at[d - 1], sum_r.at[d - 1], {"image": (x + d) % 4}))
        for d in (1, 2, 3)
    ]
    for cp in s_cp:
        cp.wait_recv()
    total = sums[0] + sums[1] + sums[2] + sums[3]
    inv = lax.rsqrt(total[0:1] * (1.0 / D) + EPS)
    inv = jnp.broadcast_to(inv, (128, 256)).T
    for j in range(16):
        t = raw[:, j * 128 : (j + 1) * 128].astype(F32)
        g = gain[pl.ds(x * 16 + j, 1), :]
        tn[x, :, j * 128 : (j + 1) * 128] = (t * inv * g).astype(BF16)

    def p_relay(n):
        p_r[n].wait_recv()
        p_r.append(go(send(prow(xl, n), prow(xl, n), ps.at[4 + n], pr.at[4 + n], right)))
        p_l[n].wait_recv()
        i = 3 - n
        p_l.append(go(send(prow(xr, i), prow(xr, i), ps.at[10 + n], pr.at[10 + n], left)))

    def trow(slot, b, half):
        return tn.at[slot, pl.ds(b * BLOCK + half * HALF, HALF)]

    t_r, t_l = [[], []], [[], []]

    def t_first(b):
        for n in (0, 1):
            piece = trow(x, b, n)
            t_r[b].append(go(send(piece, piece, ts.at[b, n], tr.at[b, n], right)))
            piece = trow(x, b, 1 - n)
            t_l[b].append(go(send(piece, piece, ts.at[b, 3 + n], tr.at[b, 3 + n], left)))

    def t_relay(b):
        t_r[b][0].wait_recv()
        piece = trow(xl, b, 0)
        t_r[b].append(go(send(piece, piece, ts.at[b, 2], tr.at[b, 2], right)))
        t_l[b][0].wait_recv()
        piece = trow(xr, b, 1)
        t_l[b].append(go(send(piece, piece, ts.at[b, 5], tr.at[b, 5], left)))

    def wkv_at(cc, p, v):
        return wkv.at[pl.ds((1 - zh) * 4096 + cc * 2048 + p * 1024, 1024), pl.ds(v * 128, 128)]

    p_relay(0)
    k2, k3 = [], []
    for v in (0, 1):
        k1[v].wait_recv()
        piece = wkv_at(c, 1 - zl, v)
        k2.append(go(send(piece, piece, ks.at[2 + v], kr.at[2 + v], near)))
        k3.append(go(send(piece, piece, ks.at[4 + v], kr.at[4 + v], sib)))
    p_relay(1)
    t_first(0)
    o_sib = []

    def o_to(cy, p, idx, dev):
        piece = wo.at[orow(cy, p)]
        return go(send(piece, piece, os.at[idx], orr.at[idx], dev))

    o1.wait_recv()
    o2 = o_to(y, 1 - zl, 1, near)
    o_r, o_l = [o_to(y, 1 - zl, 2, yr)], [o_to(y, 1 - zl, 5, yl)]
    o_sib.append(o_to(y, 1 - zl, 8, sib))
    for v in (0, 1):
        k2[v].wait_recv()
        piece = wkv_at(c, zl, v)
        k3.append(go(send(piece, piece, ks.at[6 + v], kr.at[6 + v], sib)))

    q2, q3 = [], []

    def q_pass(j):
        q1[j].wait_recv()
        piece = wq_at(1 - zh, c, 1 - zl, j)
        q2.append(go(send(piece, piece, qs.at[1, j], qr.at[1, j], near)))
        q3.append(go(send(piece, piece, qs.at[2, j], qr.at[2, j], sib)))

    def q_last(j):
        q2[j].wait_recv()
        piece = wq_at(1 - zh, c, zl, j)
        q3.append(go(send(piece, piece, qs.at[3, j], qr.at[3, j], sib)))

    q_pass(0)
    o2.wait_recv()
    o_r.append(o_to(y, zl, 3, yr))
    o_l.append(o_to(y, zl, 6, yl))
    o_sib.append(o_to(y, zl, 9, sib))

    for cp in p_r[2:] + p_l[2:] + k3:
        cp.wait_recv()
    for i in (1, 2, 3):
        local[i].wait()
    kvacc[...] = jnp.zeros_like(kvacc)

    def kv_step(i, carry):
        cols = pl.ds(pl.multiple_of(i * 1024, 1024), 1024)
        kvacc[...] += jnp.dot(pb[:, cols], wkv[cols, :], preferred_element_type=F32)
        return carry

    lax.fori_loop(0, 8, kv_step, 0)

    def block(dy, dz):
        sc, sd = at(-dy, -dz)
        return kvb.at[sc * 2 + sd]

    mine = ctx * 2 + zh
    kvb[mine, :, 0:128] = rms(kvacc[:, 0:128], kg[...]).astype(BF16)
    kvb[mine, :, 128:256] = kvacc[:, 128:256].astype(BF16)
    g_cp, h_cp = {}, []

    def g_send(sy, sz, dy, dz):
        piece, k = block(sy, sz), (sy + dy) * 4 + sz + dz
        g_cp[k] = go(send(piece, piece, gs.at[k], gr.at[k], to(dy, dz)))

    def h_send(sy, sz):
        piece, k = block(sy, sz), sy * 4 + sz
        h_cp.append(go(send(piece, piece, hs.at[k], hr.at[k], sib)))

    for dz in (1, 3, 2):
        g_send(0, 0, 0, dz)
    for dy in (1, 3):
        g_send(0, 0, dy, 0)
    h_send(0, 0)

    t_relay(0)
    t_first(1)
    q_pass(1)
    q_last(0)
    for dz in (1, 3, 2):
        g_cp[dz].wait_recv()
        for dy in (1, 3):
            g_send(0, dz, dy, 0)
        h_send(0, dz)
    o_r[0].wait_recv()
    o_r.append(o_to(y - 1, 1 - zl, 4, yr))
    o_sib.append(o_to(y - 1, 1 - zl, 10, sib))
    o_l[0].wait_recv()
    o_sib.append(o_to(y + 1, 1 - zl, 11, sib))
    q_pass(2)
    q_last(1)
    o_r[1].wait_recv()
    o_sib.append(o_to(y - 1, zl, 12, sib))
    o_l[1].wait_recv()
    o_l.append(o_to(y + 1, zl, 7, yl))
    o_sib.append(o_to(y + 1, zl, 13, sib))
    for dz in (0, 1, 3, 2):
        for dy in (1, 3):
            g_cp[dy * 4 + dz].wait_recv()
            if (dy == 1) == (dz < 2):
                g_send(dy, dz, (2 - dy), 0)
            h_send(dy, dz)
    q_pass(3)
    q_last(2)
    q_last(3)
    t_relay(1)

    def project(slot, b):
        def step(i, carry):
            cols = pl.ds(pl.multiple_of(i * 512, 512), 512)
            rows = pl.ds(pl.multiple_of((i % 2) * 512, 512), 512)
            acc[...] += jnp.dot(
                tn[slot, b * BLOCK : (b + 1) * BLOCK, cols], wq[slot * 2 + i // 2, rows, :],
                preferred_element_type=F32,
            )
            return carry

        lax.fori_loop(0, 4, step, 0)

    def queries(b):
        acc[...] = jnp.zeros_like(acc)
        project(x, b)
        t_r[b][1].wait_recv()
        project(xl, b)
        t_l[b][1].wait_recv()
        project(xr, b)
        t_r[b][2].wait_recv()
        t_l[b][2].wait_recv()
        project(xo, b)
        for h in range(8):
            v = rms(acc[:, h * HD : (h + 1) * HD], qg[...])
            qh[b, h * BLOCK : (h + 1) * BLOCK, :] = v.astype(BF16)

    local[4].wait()
    for cp in q3:
        cp.wait_recv()
    queries(0)
    for dz in (0, 1, 3, 2):
        g_cp[8 + dz].wait_recv()
        h_send(2, dz)
    o_r[2].wait_recv()
    o_sib.append(o_to(y - 2, 1 - zl, 14, sib))
    o_l[2].wait_recv()
    o_sib.append(o_to(y + 2, zl, 15, sib))
    for cp in h_cp:
        cp.wait_recv()

    def attend(b, lo, hi):
        if lo == 0:
            m[...] = jnp.full_like(m, -1e30)
            l[...] = jnp.zeros_like(l)
            a[...] = jnp.zeros_like(a)

        def step(s, carry):
            valid = mask[b, owner[s]]
            rows_s = pl.ds(pl.multiple_of(s * 32, 32), 32)

            def scores(t):
                keys = kvb[:, rows_s, 0:128].reshape(1024, 128)
                return lax.dot_general(
                    qh[b, t * 256 : (t + 1) * 256, :], keys, (((1,), (1,)), ((), ())),
                    preferred_element_type=F32,
                )

            after = scores(0)
            for t in range(4):
                rows = slice(t * 256, (t + 1) * 256)
                sc = after
                if t < 3:
                    after = scores(t + 1)
                old = m[rows, :]
                top = jnp.max(sc, axis=-1, keepdims=True) * SCALE
                new = jnp.where(valid > 0, jnp.maximum(old, top), old)
                low = jnp.where(valid > 0, new, 1e30)
                w = jnp.exp2(sc * SCALE - low[:, 0:1])
                fac = jnp.exp2(old - new)
                vals = kvb[:, rows_s, 128:256].reshape(1024, 128)
                l[rows, :] = l[rows, :] * fac + jnp.sum(w, axis=-1, keepdims=True)
                a[rows, :] = a[rows, :] * fac + jnp.dot(w.astype(BF16), vals, preferred_element_type=F32)
                m[rows, :] = new
            return carry

        lax.fori_loop(lo, hi, step, 0)
        if hi == 8:
            for h in range(8):
                rows = slice(h * BLOCK, (h + 1) * BLOCK)
                att[:, h * HD : (h + 1) * HD] = (a[rows, :] / l[rows, :]).astype(BF16)

    def give_to(b, i):
        return send(give.at[b, i], take.at[b, i], rs.at[b, i], rr.at[b, i], left if i in (1, 4, 5) else right)

    r_cp = [{}, {}]

    def product(t, store):
        def step(n, carry):
            cols = pl.ds(pl.multiple_of((n % 2) * 512, 512), 512)
            v = jnp.dot(att[...], wq[t * 2 + n // 2, :, cols], preferred_element_type=F32)
            store(pl.ds(pl.multiple_of(n * 512, 512), 512), v)
            return carry

        lax.fori_loop(0, 4, step, 0)

    def reduce_start(b):
        def far(cols, v):
            give[b, 0, :, cols] = v[0:HALF].astype(BF16)
            give[b, 1, :, cols] = v[HALF:BLOCK].astype(BF16)

        def to_right(cols, v):
            give[b, 3, :, cols] = v[HALF:BLOCK].astype(BF16)
            part[b, 0, :, cols] = v[0:HALF]

        def to_left(cols, v):
            give[b, 4, :, cols] = v[0:HALF].astype(BF16)
            part[b, 1, :, cols] = v[HALF:BLOCK]

        for t, store, slots in ((xo, far, (0, 1)), (xr, to_right, (3,)), (xl, to_left, (4,))):
            product(t, store)
            for i in slots:
                r_cp[b][i] = go(give_to(b, i))

    def reduce_relay(b):
        for k, i in ((0, 2), (1, 5)):
            r_cp[b][k].wait_recv()
            give[b, i] = (part[b, k] + take[b, k].astype(F32)).astype(BF16)
            r_cp[b][i] = go(give_to(b, i))

    def own_product(b):
        def store(cols, v):
            part[b, 0, :, cols] = v[0:HALF]
            part[b, 1, :, cols] = v[HALF:BLOCK]

        product(x, store)

    def finish(b):
        scale = jnp.tanh(jnp.full((8, 128), gate[0], F32))[0:1, 0:1]
        for k, (i, j) in enumerate(((4, 2), (3, 5))):
            r_cp[b][i].wait_recv()
            r_cp[b][j].wait_recv()
            v = part[b, k] + take[b, i].astype(F32) + take[b, j].astype(F32)
            out[b * BLOCK + k * HALF : b * BLOCK + (k + 1) * HALF] = (scale * v).astype(BF16)

    attend(0, 0, 4)
    queries(1)
    for cp in o_sib:
        cp.wait_recv()
    for cp in sends:
        cp.wait_send()
    sends.clear()
    loads = []
    for i in range(4):
        cols = pl.ds(i * 1024, 1024)
        loads.append(pltpu.make_async_copy(ow.at[:, cols], wq.at[zh * 4 + i], wload.at[i]))
        loads.append(pltpu.make_async_copy(wo.at[:, cols], wq.at[(1 - zh) * 4 + i], wload.at[4 + i]))
    for cp in loads:
        cp.start()
    attend(0, 4, 8)
    for cp in loads:
        cp.wait()
    reduce_start(0)
    attend(1, 0, 4)
    reduce_relay(0)
    own_product(0)
    attend(1, 4, 8)
    reduce_start(1)
    finish(0)
    reduce_relay(1)
    own_product(1)
    finish(1)
    for cp in sends:
        cp.wait_send()


def local(
    text, patches, in_gain, q_weight, k_weight, v_weight, o_weight, q_gain, k_gain, gate, block_mask, owner_ids
):
    dma = pltpu.SemaphoreType.DMA
    smem = pl.BlockSpec(memory_space=pltpu.SMEM)
    return pl.pallas_call(
        kernel,
        name="gated_cross_attention",
        out_shape=(
            jax.ShapeDtypeStruct((256, 2048), BF16),
            jax.ShapeDtypeStruct((1024, 4096), BF16),
        ),
        in_specs=[ANY, ANY, VMEM, ANY, ANY, ANY, ANY, VMEM, VMEM, smem, smem, smem],
        out_specs=(VMEM, ANY),
        scratch_shapes=[
            pltpu.VMEM((256, 2048), BF16),
            pltpu.VMEM((4, 256, 2048), BF16),
            pltpu.VMEM((256, D), BF16),
            pltpu.VMEM((8, 1024, 1024), BF16),
            pltpu.VMEM((D, 256), BF16),
            pltpu.VMEM((BLOCK, 1024), F32),
            pltpu.VMEM((256, 256), F32),
            pltpu.VMEM((32, 256, 256), BF16),
            pltpu.VMEM((4, 8, 256), F32),
            pltpu.VMEM((2, 1024, HD), BF16),
            pltpu.VMEM((1024, HD), F32),
            pltpu.VMEM((1024, HD), F32),
            pltpu.VMEM((1024, HD), F32),
            pltpu.VMEM((BLOCK, 1024), BF16),
            pltpu.VMEM((2, 2, HALF, 2048), F32),
            pltpu.VMEM((2, 6, HALF, 2048), BF16),
            pltpu.VMEM((2, 6, HALF, 2048), BF16),
            dma((5,)), dma((8,)), dma((3,)), dma((3,)), dma((12,)), dma((12,)), dma((2, 6)), dma((2, 6)),
            dma((8,)), dma((8,)), dma((4, NQ)), dma((4, NQ)), dma((16,)), dma((16,)),
            dma((16,)), dma((16,)), dma((16,)), dma((16,)), dma((2, 6)), dma((2, 6)),
        ],
        compiler_params=pltpu.CompilerParams(
            collective_id=0, has_side_effects=True, vmem_limit_bytes=60 << 20
        ),
    )(
        text, patches.reshape(64, D), in_gain.reshape(64, 128), q_weight.reshape(4, 1024, 1024), k_weight, v_weight,
        o_weight, q_gain.reshape(1, HD), k_gain.reshape(1, HD), gate, block_mask, owner_ids,
    )[0]


def solution(mesh):
    in_specs = (
        P(("context", "dp"), "image"),
        P("image", ("context", "dp"), None),
        P(),
        P("dp", "image"),
        P("dp", "image"),
        P("dp", "image"),
        P("image", "dp"),
        P(),
        P(),
        P(),
        P(("context", "dp"), None),
        P(),
    )
    out_specs = P(("context", "dp"), "image")
    return jax.shard_map(local, mesh=mesh, in_specs=in_specs, out_specs=out_specs, check_vma=False)
```

time: 868 us -> 180 us (0.21)
  waiting for transfers between devices: 749 us -> 0 us
  Pallas kernels: 0 us -> 176 us
  matrix products: 74.3 us -> 0 us
  other arithmetic: 27.1 us -> 0 us
  between operations: 14 us -> 0.66 us
    all_gather x8 -> x0, waiting for transfers between devices: 666 us -> none  [the longest x1 202 us: local(): lax.all_gather(q_weight, 'dp', axis=0, tiled=True)]
    pallas_call x0 -> x1, Pallas kernels: none -> 176 us  [local(): pl.pallas_call(kernel, name='gated_cross_attention', out_shape=(jax.Shape...]
    reduce_scatter x1 -> x0, waiting for transfers between devices: 79.2 us -> none  [local(): lax.psum_scatter(projected, 'image', scatter_dimension=1, tiled=True)]
    dot_general x20 -> x0, matrix products: 74.3 us -> none  [the longest x8 25.4 us: one_group(): jnp.einsum('tjd,irjd->jtir', group_queries, key_piece, preferred_element_...]
    reduce_sum x11 -> x0, other arithmetic: 22.9 us -> none  [the longest x8 19.4 us: one_group(): new_total = running_total * factor + jnp.sum(weights, axis=(2, 3))]
  transfers between devices with their start and end apart: 9 -> 0, of which waited for: 9 -> 0; matrix products, arithmetic and copies ran while one was open for 10% -> 0% of each run, Pallas kernels for 0% -> 0%
where the time goes in v2:
time: 180 us; the launch traced here: 179 us
  Pallas kernels  176 us (98%)
  local copies, waits for them, and re-layouts  2.3 us (1%)
    pallas_call x1, Pallas kernels, local(): pl.pallas_call(kernel, name='gated_cross_attention', out_shape=(jax.Shape...  176 us

profile of v2, /device:TPU:1, one launch (start us, length us, event | category | flops | bytes accessed | tf_op | source)
XLA Modules:
  0.0 178.6 jit_solution(9637520863072902088)
XLA Ops:
  0.7 175.6 %gated_cross_attention.1 = (bf16[256,2048]{1,0:T(8,128)(2,1)}, bf16[1024,4096]{1,0:T(8,128)(2,1)}) custom-call(bf16[256,2048]{1,0:T(8,128)(2,1)} %text.1, bf16[64,8192]{1,0:T(8,128)(2,1)} %bitcast.6, f32[64,128]{1,0:T(8,128)} %bitcast.7, bf16[4,1024,1024]{2,1,0:T(8,128)(2,1)} %bitcast.5, bf16[4096,128]{1,0:T(8,128)(2,1)} %kw.1, bf16[4096,128]{1,0:T(8,128)(2,1)} %vw.1, ...), custom_call_target="tpu_custom_call" | custom-call | tf_op jit(solution)/shard_map/gated_cross_attention/pallas_call | solution.py:456
  176.3 2.3 %copy.15 = bf16[256,2048]{1,0:T(8,128)(2,1)} copy(bf16[256,2048]{1,0:T(8,128)(2,1)} %get-tuple-element.6) | data formatting | bytes 2097152

commit v3 on v2

--- a/solution.py
+++ b/solution.py
@@ -14,7 +14,6 @@
 HD = 128
 BLOCK = 128
 EPS = 1e-05
-NQ = 4
 HALF = 64
 LOG2E = 1.4426950408889634
 SCALE = LOG2E / HD**0.5
@@ -42,7 +41,7 @@
     text, patches, gain, qw, kw, vw, ow, qg, kg, gate, mask, owner,
     out, wo,
     raw, tn, pb, wq, wkv, acc, kvacc, kvb, sums, qh, m, l, a, att, part, give, take,
-    loc, wload, sum_s, sum_r, ps, pr, ts, tr, ks, kr, qs, qr, os, orr, gs, gr, hs, hr, rs, rr,
+    loc, wload, sum_s, sum_r, ps, pr, ts, tr, ks, kr, qs, qr, ys, yrr, os, orr, gs, gr, hs, hr, rs, rr,
 ):
     x, y, zh, zl, c = place()
     ctx = lax.axis_index("context")
@@ -97,28 +96,71 @@
     p_r, p_l = [], []
     p_first(0)
 
+    class Round:
+        def __init__(self, source, piece, ss, rr):
+            self.piece, self.ss, self.rr = piece, ss, rr
+            self.first = go(send(source, piece(zh, c, y, zl), ss.at[0], rr.at[0], cross))
+            self.r, self.l, self.s = [], [], []
+
+        def on(self, dy, p, idx, dev):
+            piece = self.piece(1 - zh, c, (y + dy + 4) % 4, p)
+            return go(send(piece, piece, self.ss.at[idx], self.rr.at[idx], dev))
+
+        def crossed(self):
+            self.first.wait_recv()
+            self.near = self.on(0, 1 - zl, 1, near)
+            self.r.append(self.on(0, 1 - zl, 2, yr))
+            self.l.append(self.on(0, 1 - zl, 5, yl))
+            self.s.append(self.on(0, 1 - zl, 8, sib))
+
+        def neared(self):
+            self.near.wait_recv()
+            self.r.append(self.on(0, zl, 3, yr))
+            self.l.append(self.on(0, zl, 6, yl))
+            self.s.append(self.on(0, zl, 9, sib))
+
+        def y_first(self):
+            self.r[0].wait_recv()
+            self.r.append(self.on(-1, 1 - zl, 4, yr))
+            self.s.append(self.on(-1, 1 - zl, 10, sib))
+            self.l[0].wait_recv()
+            self.s.append(self.on(1, 1 - zl, 11, sib))
+
+        def y_second(self):
+            self.l[1].wait_recv()
+            self.l.append(self.on(1, zl, 7, yl))
+            self.s.append(self.on(1, zl, 13, sib))
+            self.r[1].wait_recv()
+            self.s.append(self.on(-1, zl, 12, sib))
+
+        def y_far(self):
+            self.r[2].wait_recv()
+            self.s.append(self.on(-2, 1 - zl, 14, sib))
+            self.l[2].wait_recv()
+            self.s.append(self.on(2, zl, 15, sib))
+
+        def end(self):
+            for cp in self.s:
+                cp.wait_recv()
+
+    qy = Round(
+        qw.at[c * 2 + zl, pl.ds(512 + y * 128, 128)],
+        lambda h, cc, cy, p: wq.at[h * 4 + cc * 2 + p, pl.ds(512 + cy * 128, 128)], ys, yrr,
+    )
+
     rows_mine = pl.ds(c * 2048 + zl * 1024, 1024)
     rows_there = pl.ds(zh * 4096 + c * 2048 + zl * 1024, 1024)
     k1 = [
         go(send(kw.at[rows_mine], wkv.at[rows_there, pl.ds(0, 128)], ks.at[0], kr.at[0], cross)),
         go(send(vw.at[rows_mine], wkv.at[rows_there, pl.ds(128, 128)], ks.at[1], kr.at[1], cross)),
     ]
-    for n in (1, 2, 3):
-        p_first(n)
-
-    def orow(cy, p):
-        return pl.ds(c * 512 + ((cy + 4) % 4) * 128 + p * 64, 64)
-
-    o1 = go(send(ow.at[orow(y, zl)], wo.at[orow(y, zl)], os.at[0], orr.at[0], cross))
-
-    rows_q = 1024 // NQ
 
     def wq_at(h, cc, p, j):
-        return wq.at[h * 4 + cc * 2 + p, pl.ds(j * rows_q, rows_q)]
+        return wq.at[h * 4 + cc * 2 + p, pl.ds(j * 256, 256)]
 
     q1 = [
-        go(send(qw.at[c * 2 + zl, pl.ds(j * rows_q, rows_q)], wq_at(zh, c, zl, j), qs.at[0, j], qr.at[0, j], cross))
-        for j in range(NQ)
+        go(send(qw.at[c * 2 + zl, pl.ds(j * 256, 256)], wq_at(zh, c, zl, j), qs.at[0, j], qr.at[0, j], cross))
+        for j in range(2)
     ]
 
     local[0].wait()
@@ -132,6 +174,18 @@
         go(send(sums.at[x], sums.at[x], sum_s.at[d - 1], sum_r.at[d - 1], {"image": (x + d) % 4}))
         for d in (1, 2, 3)
     ]
+    for n in (1, 2, 3):
+        p_first(n)
+
+    def p_relay(n):
+        p_r[n].wait_recv()
+        p_r.append(go(send(prow(xl, n), prow(xl, n), ps.at[4 + n], pr.at[4 + n], right)))
+        p_l[n].wait_recv()
+        i = 3 - n
+        p_l.append(go(send(prow(xr, i), prow(xr, i), ps.at[10 + n], pr.at[10 + n], left)))
+
+    qy.crossed()
+    p_relay(0)
     for cp in s_cp:
         cp.wait_recv()
     total = sums[0] + sums[1] + sums[2] + sums[3]
@@ -142,13 +196,6 @@
         g = gain[pl.ds(x * 16 + j, 1), :]
         tn[x, :, j * 128 : (j + 1) * 128] = (t * inv * g).astype(BF16)
 
-    def p_relay(n):
-        p_r[n].wait_recv()
-        p_r.append(go(send(prow(xl, n), prow(xl, n), ps.at[4 + n], pr.at[4 + n], right)))
-        p_l[n].wait_recv()
-        i = 3 - n
-        p_l.append(go(send(prow(xr, i), prow(xr, i), ps.at[10 + n], pr.at[10 + n], left)))
-
     def trow(slot, b, half):
         return tn.at[slot, pl.ds(b * BLOCK + half * HALF, HALF)]
 
@@ -172,25 +219,17 @@
     def wkv_at(cc, p, v):
         return wkv.at[pl.ds((1 - zh) * 4096 + cc * 2048 + p * 1024, 1024), pl.ds(v * 128, 128)]
 
-    p_relay(0)
+    p_relay(1)
+    t_first(0)
+    qy.neared()
     k2, k3 = [], []
     for v in (0, 1):
         k1[v].wait_recv()
         piece = wkv_at(c, 1 - zl, v)
         k2.append(go(send(piece, piece, ks.at[2 + v], kr.at[2 + v], near)))
         k3.append(go(send(piece, piece, ks.at[4 + v], kr.at[4 + v], sib)))
-    p_relay(1)
-    t_first(0)
-    o_sib = []
-
-    def o_to(cy, p, idx, dev):
-        piece = wo.at[orow(cy, p)]
-        return go(send(piece, piece, os.at[idx], orr.at[idx], dev))
-
-    o1.wait_recv()
-    o2 = o_to(y, 1 - zl, 1, near)
-    o_r, o_l = [o_to(y, 1 - zl, 2, yr)], [o_to(y, 1 - zl, 5, yl)]
-    o_sib.append(o_to(y, 1 - zl, 8, sib))
+    qy.y_first()
+    qy.y_second()
     for v in (0, 1):
         k2[v].wait_recv()
         piece = wkv_at(c, zl, v)
@@ -210,10 +249,6 @@
         q3.append(go(send(piece, piece, qs.at[3, j], qr.at[3, j], sib)))
 
     q_pass(0)
-    o2.wait_recv()
-    o_r.append(o_to(y, zl, 3, yr))
-    o_l.append(o_to(y, zl, 6, yl))
-    o_sib.append(o_to(y, zl, 9, sib))
 
     for cp in p_r[2:] + p_l[2:] + k3:
         cp.wait_recv()
@@ -253,35 +288,26 @@
 
     t_relay(0)
     t_first(1)
-    q_pass(1)
-    q_last(0)
+    qy.y_far()
     for dz in (1, 3, 2):
         g_cp[dz].wait_recv()
         for dy in (1, 3):
             g_send(0, dz, dy, 0)
         h_send(0, dz)
-    o_r[0].wait_recv()
-    o_r.append(o_to(y - 1, 1 - zl, 4, yr))
-    o_sib.append(o_to(y - 1, 1 - zl, 10, sib))
-    o_l[0].wait_recv()
-    o_sib.append(o_to(y + 1, 1 - zl, 11, sib))
-    q_pass(2)
-    q_last(1)
-    o_r[1].wait_recv()
-    o_sib.append(o_to(y - 1, zl, 12, sib))
-    o_l[1].wait_recv()
-    o_l.append(o_to(y + 1, zl, 7, yl))
-    o_sib.append(o_to(y + 1, zl, 13, sib))
+    q_last(0)
+    q_pass(1)
+    wide = Round(
+        ow.at[pl.ds(c * 512 + y * 128 + zl * 64, 64)],
+        lambda h, cc, cy, p: wo.at[pl.ds(cc * 512 + cy * 128 + p * 64, 64)], os, orr,
+    )
     for dz in (0, 1, 3, 2):
         for dy in (1, 3):
             g_cp[dy * 4 + dz].wait_recv()
             if (dy == 1) == (dz < 2):
                 g_send(dy, dz, (2 - dy), 0)
             h_send(dy, dz)
-    q_pass(3)
-    q_last(2)
-    q_last(3)
     t_relay(1)
+    q_last(1)
 
     def project(slot, b):
         def step(i, carry):
@@ -312,14 +338,13 @@
     local[4].wait()
     for cp in q3:
         cp.wait_recv()
+    qy.end()
     queries(0)
+    wide.crossed()
     for dz in (0, 1, 3, 2):
         g_cp[8 + dz].wait_recv()
         h_send(2, dz)
-    o_r[2].wait_recv()
-    o_sib.append(o_to(y - 2, 1 - zl, 14, sib))
-    o_l[2].wait_recv()
-    o_sib.append(o_to(y + 2, zl, 15, sib))
+    wide.neared()
     for cp in h_cp:
         cp.wait_recv()
 
@@ -362,17 +387,17 @@
         if hi == 8:
             for h in range(8):
                 rows = slice(h * BLOCK, (h + 1) * BLOCK)
-                att[:, h * HD : (h + 1) * HD] = (a[rows, :] / l[rows, :]).astype(BF16)
+                att[b, :, h * HD : (h + 1) * HD] = (a[rows, :] / l[rows, :]).astype(BF16)
 
     def give_to(b, i):
         return send(give.at[b, i], take.at[b, i], rs.at[b, i], rr.at[b, i], left if i in (1, 4, 5) else right)
 
     r_cp = [{}, {}]
 
-    def product(t, store):
+    def product(b, t, store):
         def step(n, carry):
             cols = pl.ds(pl.multiple_of((n % 2) * 512, 512), 512)
-            v = jnp.dot(att[...], wq[t * 2 + n // 2, :, cols], preferred_element_type=F32)
+            v = jnp.dot(att[b], wq[t * 2 + n // 2, :, cols], preferred_element_type=F32)
             store(pl.ds(pl.multiple_of(n * 512, 512), 512), v)
             return carry
 
@@ -392,7 +417,7 @@
             part[b, 1, :, cols] = v[HALF:BLOCK]
 
         for t, store, slots in ((xo, far, (0, 1)), (xr, to_right, (3,)), (xl, to_left, (4,))):
-            product(t, store)
+            product(b, t, store)
             for i in slots:
                 r_cp[b][i] = go(give_to(b, i))
 
@@ -407,7 +432,7 @@
             part[b, 0, :, cols] = v[0:HALF]
             part[b, 1, :, cols] = v[HALF:BLOCK]
 
-        product(x, store)
+        product(b, x, store)
 
     def finish(b):
         scale = jnp.tanh(jnp.full((8, 128), gate[0], F32))[0:1, 0:1]
@@ -417,10 +442,15 @@
             v = part[b, k] + take[b, i].astype(F32) + take[b, j].astype(F32)
             out[b * BLOCK + k * HALF : b * BLOCK + (k + 1) * HALF] = (scale * v).astype(BF16)
 
-    attend(0, 0, 4)
+    attend(0, 0, 2)
+    wide.y_first()
+    attend(0, 2, 4)
+    wide.y_second()
     queries(1)
-    for cp in o_sib:
-        cp.wait_recv()
+    attend(0, 4, 6)
+    wide.y_far()
+    attend(0, 6, 8)
+    wide.end()
     for cp in sends:
         cp.wait_send()
     sends.clear()
@@ -431,11 +461,11 @@
         loads.append(pltpu.make_async_copy(wo.at[:, cols], wq.at[(1 - zh) * 4 + i], wload.at[4 + i]))
     for cp in loads:
         cp.start()
-    attend(0, 4, 8)
+    attend(1, 0, 2)
     for cp in loads:
         cp.wait()
     reduce_start(0)
-    attend(1, 0, 4)
+    attend(1, 2, 4)
     reduce_relay(0)
     own_product(0)
     attend(1, 4, 8)
@@ -476,12 +506,12 @@
             pltpu.VMEM((1024, HD), F32),
             pltpu.VMEM((1024, HD), F32),
             pltpu.VMEM((1024, HD), F32),
-            pltpu.VMEM((BLOCK, 1024), BF16),
+            pltpu.VMEM((2, BLOCK, 1024), BF16),
             pltpu.VMEM((2, 2, HALF, 2048), F32),
             pltpu.VMEM((2, 6, HALF, 2048), BF16),
             pltpu.VMEM((2, 6, HALF, 2048), BF16),
             dma((5,)), dma((8,)), dma((3,)), dma((3,)), dma((12,)), dma((12,)), dma((2, 6)), dma((2, 6)),
-            dma((8,)), dma((8,)), dma((4, NQ)), dma((4, NQ)), dma((16,)), dma((16,)),
+            dma((8,)), dma((8,)), dma((4, 2)), dma((4, 2)), dma((16,)), dma((16,)), dma((16,)), dma((16,)),
             dma((16,)), dma((16,)), dma((16,)), dma((16,)), dma((2, 6)), dma((2, 6)),
         ],
         compiler_params=pltpu.CompilerParams(

time: 180 us -> 167 us (0.928)
  Pallas kernels: 176 us -> 163 us
    pallas_call x1, Pallas kernels: 176 us -> 163 us  [local(): pl.pallas_call(kernel, name='gated_cross_attention', out_shape=(jax.Shape...]
where the time goes in v3:
time: 167 us; the launch traced here: 166 us
  Pallas kernels  163 us (98%)
  local copies, waits for them, and re-layouts  2.3 us (1%)
    pallas_call x1, Pallas kernels, local(): pl.pallas_call(kernel, name='gated_cross_attention', out_shape=(jax.Shape...  163 us

profile of v3, /device:TPU:1, one launch (start us, length us, event | category | flops | bytes accessed | tf_op | source)
XLA Modules:
  0.0 165.7 jit_solution(5999218638582432920)
XLA Ops:
  0.7 162.7 %gated_cross_attention.1 = (bf16[256,2048]{1,0:T(8,128)(2,1)}, bf16[1024,4096]{1,0:T(8,128)(2,1)}) custom-call(bf16[256,2048]{1,0:T(8,128)(2,1)} %text.1, bf16[64,8192]{1,0:T(8,128)(2,1)} %bitcast.6, f32[64,128]{1,0:T(8,128)} %bitcast.7, bf16[4,1024,1024]{2,1,0:T(8,128)(2,1)} %bitcast.5, bf16[4096,128]{1,0:T(8,128)(2,1)} %kw.1, bf16[4096,128]{1,0:T(8,128)(2,1)} %vw.1, ...), custom_call_target="tpu_custom_call" | custom-call | tf_op jit(solution)/shard_map/gated_cross_attention/pallas_call | solution.py:486
  163.3 2.3 %copy.15 = bf16[256,2048]{1,0:T(8,128)(2,1)} copy(bf16[256,2048]{1,0:T(8,128)(2,1)} %get-tuple-element.6) | data formatting | bytes 2097152

commit v4 on v3

--- a/solution.py
+++ b/solution.py
@@ -39,9 +39,9 @@
 
 def kernel(
     text, patches, gain, qw, kw, vw, ow, qg, kg, gate, mask, owner,
-    out, wo,
-    raw, tn, pb, wq, wkv, acc, kvacc, kvb, sums, qh, m, l, a, att, part, give, take,
-    loc, wload, sum_s, sum_r, ps, pr, ts, tr, ks, kr, qs, qr, ys, yrr, os, orr, gs, gr, hs, hr, rs, rr,
+    out,
+    wo, raw, tn, pb, wq, wkv, acc, kvacc, kvb, sums, qh, m, l, a, att, part, give, take,
+    loc, wload, sum_s, sum_r, ps, pr, ts, tr, ks, kr, qs, qr, ys, yrr, zs, zr, os, orr, gs, gr, hs, hr, rs, rr,
 ):
     x, y, zh, zl, c = place()
     ctx = lax.axis_index("context")
@@ -154,6 +154,29 @@
         go(send(kw.at[rows_mine], wkv.at[rows_there, pl.ds(0, 128)], ks.at[0], kr.at[0], cross)),
         go(send(vw.at[rows_mine], wkv.at[rows_there, pl.ds(128, 128)], ks.at[1], kr.at[1], cross)),
     ]
+
+    class Pair:
+        def __init__(self, sources, piece, ss, rr):
+            self.piece, self.ss, self.rr = piece, ss, rr
+            self.first = [
+                go(send(src, piece(zh, c, zl, j), ss.at[0, j], rr.at[0, j], cross)) for j, src in enumerate(sources)
+            ]
+            self.near, self.s = {}, []
+
+        def crossed(self, j):
+            self.first[j].wait_recv()
+            piece = self.piece(1 - zh, c, 1 - zl, j)
+            self.near[j] = go(send(piece, piece, self.ss.at[1, j], self.rr.at[1, j], near))
+            self.s.append(go(send(piece, piece, self.ss.at[2, j], self.rr.at[2, j], sib)))
+
+        def neared(self, j):
+            self.near[j].wait_recv()
+            piece = self.piece(1 - zh, c, zl, j)
+            self.s.append(go(send(piece, piece, self.ss.at[3, j], self.rr.at[3, j], sib)))
+
+        def end(self):
+            for cp in self.s:
+                cp.wait_recv()
 
     def wq_at(h, cc, p, j):
         return wq.at[h * 4 + cc * 2 + p, pl.ds(j * 256, 256)]
@@ -294,12 +317,16 @@
         for dy in (1, 3):
             g_send(0, dz, dy, 0)
         h_send(0, dz)
+    oy = Round(
+        ow.at[pl.ds(c * 512 + zl * 256 + 128 + y * 32, 32)],
+        lambda h, cc, cy, p: wo.at[pl.ds(cc * 512 + p * 256 + 128 + cy * 32, 32)], os, orr,
+    )
+    oz = Pair(
+        [ow.at[pl.ds(c * 512 + zl * 256 + j * 64, 64)] for j in (0, 1)],
+        lambda h, cc, p, j: wo.at[pl.ds(cc * 512 + p * 256 + j * 64, 64)], zs, zr,
+    )
     q_last(0)
     q_pass(1)
-    wide = Round(
-        ow.at[pl.ds(c * 512 + y * 128 + zl * 64, 64)],
-        lambda h, cc, cy, p: wo.at[pl.ds(cc * 512 + cy * 128 + p * 64, 64)], os, orr,
-    )
     for dz in (0, 1, 3, 2):
         for dy in (1, 3):
             g_cp[dy * 4 + dz].wait_recv()
@@ -308,6 +335,7 @@
             h_send(dy, dz)
     t_relay(1)
     q_last(1)
+    oy.crossed()
 
     def project(slot, b):
         def step(i, carry):
@@ -340,11 +368,11 @@
         cp.wait_recv()
     qy.end()
     queries(0)
-    wide.crossed()
+    oz.crossed(0)
     for dz in (0, 1, 3, 2):
         g_cp[8 + dz].wait_recv()
         h_send(2, dz)
-    wide.neared()
+    oy.neared()
     for cp in h_cp:
         cp.wait_recv()
 
@@ -442,15 +470,18 @@
             v = part[b, k] + take[b, i].astype(F32) + take[b, j].astype(F32)
             out[b * BLOCK + k * HALF : b * BLOCK + (k + 1) * HALF] = (scale * v).astype(BF16)
 
+    oz.crossed(1)
     attend(0, 0, 2)
-    wide.y_first()
+    oy.y_first()
+    oy.y_second()
     attend(0, 2, 4)
-    wide.y_second()
+    oz.neared(0)
+    oy.y_far()
     queries(1)
-    attend(0, 4, 6)
-    wide.y_far()
-    attend(0, 6, 8)
-    wide.end()
+    oz.neared(1)
+    attend(0, 4, 8)
+    oy.end()
+    oz.end()
     for cp in sends:
         cp.wait_send()
     sends.clear()
@@ -465,10 +496,10 @@
     for cp in loads:
         cp.wait()
     reduce_start(0)
-    attend(1, 2, 4)
+    attend(1, 2, 5)
     reduce_relay(0)
     own_product(0)
-    attend(1, 4, 8)
+    attend(1, 5, 8)
     reduce_start(1)
     finish(0)
     reduce_relay(1)
@@ -486,13 +517,11 @@
     return pl.pallas_call(
         kernel,
         name="gated_cross_attention",
-        out_shape=(
-            jax.ShapeDtypeStruct((256, 2048), BF16),
-            jax.ShapeDtypeStruct((1024, 4096), BF16),
-        ),
+        out_shape=jax.ShapeDtypeStruct((256, 2048), BF16),
         in_specs=[ANY, ANY, VMEM, ANY, ANY, ANY, ANY, VMEM, VMEM, smem, smem, smem],
-        out_specs=(VMEM, ANY),
+        out_specs=VMEM,
         scratch_shapes=[
+            pltpu.VMEM((1024, 4096), BF16),
             pltpu.VMEM((256, 2048), BF16),
             pltpu.VMEM((4, 256, 2048), BF16),
             pltpu.VMEM((256, D), BF16),
@@ -511,7 +540,7 @@
             pltpu.VMEM((2, 6, HALF, 2048), BF16),
             pltpu.VMEM((2, 6, HALF, 2048), BF16),
             dma((5,)), dma((8,)), dma((3,)), dma((3,)), dma((12,)), dma((12,)), dma((2, 6)), dma((2, 6)),
-            dma((8,)), dma((8,)), dma((4, 2)), dma((4, 2)), dma((16,)), dma((16,)), dma((16,)), dma((16,)),
+            dma((8,)), dma((8,)), dma((4, 2)), dma((4, 2)), dma((16,)), dma((16,)), dma((4, 2)), dma((4, 2)), dma((16,)), dma((16,)),
             dma((16,)), dma((16,)), dma((16,)), dma((16,)), dma((2, 6)), dma((2, 6)),
         ],
         compiler_params=pltpu.CompilerParams(
@@ -520,7 +549,7 @@
     )(
         text, patches.reshape(64, D), in_gain.reshape(64, 128), q_weight.reshape(4, 1024, 1024), k_weight, v_weight,
         o_weight, q_gain.reshape(1, HD), k_gain.reshape(1, HD), gate, block_mask, owner_ids,
-    )[0]
+    )
 
 
 def solution(mesh):

time: 167 us -> 155 us (0.928)
  Pallas kernels: 163 us -> 151 us
    pallas_call x1, Pallas kernels: 163 us -> 151 us  [local(): pl.pallas_call(kernel, name='gated_cross_attention', out_shape=jax.ShapeD...]
where the time goes in v4:
time: 155 us; the launch traced here: 154 us
  Pallas kernels  151 us (97%)
  local copies, waits for them, and re-layouts  2.3 us (1%)
    pallas_call x1, Pallas kernels, local(): pl.pallas_call(kernel, name='gated_cross_attention', out_shape=jax.ShapeD...  151 us

profile of v4, /device:TPU:1, one launch (start us, length us, event | category | flops | bytes accessed | tf_op | source)
XLA Modules:
  0.0 153.9 jit_solution(375471874453036067)
XLA Ops:
  0.7 150.9 %gated_cross_attention.1 = bf16[256,2048]{1,0:T(8,128)(2,1)} custom-call(bf16[256,2048]{1,0:T(8,128)(2,1)} %text.1, bf16[64,8192]{1,0:T(8,128)(2,1)} %bitcast.6, f32[64,128]{1,0:T(8,128)} %bitcast.7, bf16[4,1024,1024]{2,1,0:T(8,128)(2,1)} %bitcast.5, bf16[4096,128]{1,0:T(8,128)(2,1)} %kw.1, bf16[4096,128]{1,0:T(8,128)(2,1)} %vw.1, bf16[1024,4096]{1,0:T(8,128)(2,1)} %ow.1, ...), custom_call_target="tpu_custom_call" | custom-call | tf_op jit(solution)/shard_map/gated_cross_attention/pallas_call | solution.py:517
  151.6 2.3 %copy.15 = bf16[256,2048]{1,0:T(8,128)(2,1)} copy(bf16[256,2048]{1,0:T(8,128)(2,1)} %gated_cross_attention.1) | data formatting | bytes 2097152
